TPU v7x, 256 devices: a whole 4x4x8 slice. The times are simulated.
256 devices in a mesh: row: 16 (over y_hi, z), col: 4 (over y_lo, core), ka: 4 (over x).
Axes of the slice: x: 4, y: 4 (y_hi: 2, y_lo: 2; y = y_hi * 2 + y_lo), z: 8, core: 2. Of those that a mesh axis runs over, the one named last changes fastest.
Arguments:
- density: bfloat16 [4096, 4096], P('row', ('col', 'ka')), may hold values from -0.375 to 0.375
- pattern_start: int32 [16, 16], replicated, may hold values from 0 to 1, as said below
- pattern_square: int32 [16, 16], replicated, may hold values from 0 to 1, as said below
Outputs:
- purified: bfloat16 [4096, 4096], P('row', ('col', 'ka'))
Inputs may be any that keep to these rules, and one draw needn't show every extreme that they name: `pattern_start`: symmetric 0/1 pattern with ones on the diagonal; the share of ones varies strongly between block rows. `pattern_square`: symmetric 0/1 pattern with ones on the diagonal; the share of ones varies strongly between block rows.
All inputs are finite; a program needn't handle non-finite values.
Results may differ from a plain program's by a relative error of at most 0.0048.
Values may be sent and summed in bfloat16 or wider, within the bound.
A program may use at most 64 MiB of HBM per device.

v0:
```python
import jax
import jax.numpy as jnp
from jax import lax
from jax.sharding import PartitionSpec as P

BLOCK = 256
STEPS = 2


def spread(shard, axis, root):
    mine = lax.axis_index(axis) == root
    return lax.psum(jnp.where(mine, shard, jnp.zeros_like(shard)), axis)


def tile_mask(pattern, row_start, col_start, row_count, col_count):
    window = lax.dynamic_slice(pattern, (row_start, col_start), (row_count, col_count))
    full = jnp.broadcast_to(window[:, None, :, None], (row_count, BLOCK, col_count, BLOCK))
    return full.reshape(row_count * BLOCK, col_count * BLOCK) == 1


def local(density, pattern_start, pattern_square):
    total_blocks = pattern_start.shape[0]
    row_blocks = density.shape[0] // BLOCK
    col_blocks = density.shape[1] // BLOCK
    col_count = lax.axis_size("col")
    inner_count = lax.axis_size("ka")
    row_index = lax.axis_index("row")
    col_index = lax.axis_index("col")
    inner_index = lax.axis_index("ka")
    out_blocks = total_blocks // col_count
    row_start = row_index * row_blocks
    col_start = (col_index * inner_count + inner_index) * col_blocks
    start_mask = tile_mask(pattern_start, row_start, col_start, row_blocks, col_blocks)
    square_mask = tile_mask(pattern_square, row_start, col_start, row_blocks, col_blocks)
    current = jnp.where(start_mask, density, jnp.zeros_like(density))
    run_length = min(row_blocks, out_blocks)
    pieces = out_blocks // run_length
    for section in range(STEPS):
        row_panel = lax.all_gather(current, "col", axis=1, tiled=True)
        received = []
        for piece_index in range(pieces):
            first_block = col_index * out_blocks + piece_index * run_length
            root_row = first_block // row_blocks
            received.append(spread(row_panel, "row", root_row))
        column_rows = jnp.concatenate(received, axis=0)
        inner_width = row_panel.shape[1]
        grouped = column_rows.reshape(1 * lax.axis_size("ka"), col_blocks * BLOCK, inner_width)
        summed = lax.psum_scatter(
            jnp.einsum("ik,qjk->qij", row_panel, grouped, preferred_element_type=jnp.float32),
            "ka",
            scatter_dimension=0,
            tiled=True,
        )[0]
        square = jnp.where(square_mask, summed, jnp.float32(0.0))
        if section % 2 == 0:
            following = 2.0 * current.astype(jnp.float32) - square
        else:
            following = square
        current = following.astype(jnp.bfloat16)
    return current


def solution(mesh):
    return jax.shard_map(
        local,
        mesh=mesh,
        in_specs=(P("row", ("col", "ka")), P(), P()),
        out_specs=P("row", ("col", "ka")),
        check_vma=False,
    )
```

profile of v0, /device:TPU:1, one launch (start us, length us, event | category | flops | bytes accessed | tf_op | source)
XLA Modules:
  0.0 416.7 jit_solution(4146122474863585654)
XLA Ops:
  6.5 0.0 all-reduce.7.cloned.1.call-start
  6.5 1.3 dynamic_slice.7
  8.5 0.9 broadcast_select_fusion.8
  9.4 9.6 %all_gather.6 = bf16[256,1024]{1,0:T(8,128)(2,1)S(1)} all-gather(bf16[256,256]{1,0:T(8,128)(2,1)S(1)} %broadcast_select_fusion.8), channel_id=1, replica_groups=mesh['row'=16,'col'=4,'ka'=4] {'col'}, dimensions={1}, use_global_device_ids=true | all-gather | bytes 655360 | tf_op jit(solution)/shard_map/all_gather | solution.py:39
  19.0 1.4 broadcast_select_fusion.7
  20.3 0.0 all-reduce.7.cloned.1.call-update
  20.4 0.0 reduce-scatter.3.cloned.1.call-start
  20.4 153.9 %all-reduce.7.cloned.1.call-done = (bf16[256,1024]{1,0:T(8,128)(2,1)}, bf16[256,1024]{1,0:T(8,128)(2,1)}, bf16[256,1024]{1,0:T(8,128)(2,1)}, bf16[256,1024]{1,0:T(8,128)(2,1)}) async-done(((bf16[256,1024]{1,0:T(8,128)(2,1)}, bf16[256,1024]{1,0:T(8,128)(2,1)}, bf16[256,1024]{1,0:T(8,128)(2,1)}, bf16[256,1024]{1,0:T(8,128)(2,1)}), (bf16[256,1024]{1,0:T(8,128)(2,1)}, bf16[256,1024]{1,0:T(8,128)(2,1)}, ...) | async-done | bytes 2097168 | tf_op jit(solution)/shard_map/psum | solution.py:12
  174.3 1.7 pad_maximum_fusion
  176.0 0.0 copy-start
  176.0 1.7 convolution_bitcast_fusion.1
  177.7 0.0 reduce-scatter.3.cloned.1.call-update
  177.8 0.0 all-reduce.5.cloned.1.call-start
  177.8 1.3 dynamic_slice.6
  179.7 30.3 %reduce-scatter.3.cloned.1.call-done = f32[1,256,256]{2,1,0:T(8,128)} async-done(((f32[4,256,256]{2,1,0:T(8,128)}), f32[1,256,256]{2,1,0:T(8,128)}) %reduce-scatter.3.cloned.1.call-update) | async-done | bytes 262160 | tf_op jit(solution)/shard_map/reduce_scatter | solution.py:48
  210.0 0.0 copy-done
  210.0 0.1 fusion.2
  210.1 10.0 %all_gather.7 = bf16[256,1024]{1,0:T(8,128)(2,1)S(1)} all-gather(bf16[256,256]{1,0:T(8,128)(2,1)S(1)} %fusion.2), channel_id=1, replica_groups=mesh['row'=16,'col'=4,'ka'=4] {'col'}, dimensions={1}, use_global_device_ids=true | all-gather | bytes 655360 | tf_op jit(solution)/shard_map/all_gather | solution.py:39
  220.1 1.4 broadcast_select_fusion.6
  221.5 0.0 all-reduce.5.cloned.1.call-update
  221.5 0.0 reduce-scatter.5.cloned.1.call-start
  221.5 152.2 %all-reduce.5.cloned.1.call-done = (bf16[256,1024]{1,0:T(8,128)(2,1)}, bf16[256,1024]{1,0:T(8,128)(2,1)}, bf16[256,1024]{1,0:T(8,128)(2,1)}, bf16[256,1024]{1,0:T(8,128)(2,1)}) async-done(((bf16[256,1024]{1,0:T(8,128)(2,1)}, bf16[256,1024]{1,0:T(8,128)(2,1)}, bf16[256,1024]{1,0:T(8,128)(2,1)}, bf16[256,1024]{1,0:T(8,128)(2,1)}), (bf16[256,1024]{1,0:T(8,128)(2,1)}, bf16[256,1024]{1,0:T(8,128)(2,1)}, ...) | async-done | bytes 2097168 | tf_op jit(solution)/shard_map/psum | solution.py:12
  373.7 1.7 pad_maximum_fusion.1
  375.4 1.7 convolution_bitcast_fusion
  377.1 0.0 reduce-scatter.5.cloned.1.call-update
  377.1 32.4 %reduce-scatter.5.cloned.1.call-done = f32[1,256,256]{2,1,0:T(8,128)} async-done(((f32[4,256,256]{2,1,0:T(8,128)}), f32[1,256,256]{2,1,0:T(8,128)}) %reduce-scatter.5.cloned.1.call-update) | async-done | bytes 262160 | tf_op jit(solution)/shard_map/reduce_scatter | solution.py:48
  409.5 0.7 fusion.3
Async XLA Ops:
  6.5 167.8 %all-reduce.7.cloned.1.call-start = ((), (), s32[]{:S(2)}) async-start(), calls=%async_computation.5 | async-start | bytes 4194304 | tf_op jit(solution)/shard_map/psum | solution.py:12
  20.4 189.7 %reduce-scatter.3.cloned.1.call-start = ((), (), s32[]{:S(2)}) async-start(), calls=%async_computation.2 | async-start | bytes 1310720 | tf_op jit(solution)/shard_map/reduce_scatter | solution.py:48
  176.0 34.0 %copy-start = (bf16[256,256]{1,0:T(8,128)(2,1)S(1)}, bf16[256,256]{1,0:T(8,128)(2,1)}, u32[]{:S(2)}) copy-start(bf16[256,256]{1,0:T(8,128)(2,1)} %param.3) | copy-start | bytes 393220
  177.8 196.0 %all-reduce.5.cloned.1.call-start = ((), (), s32[]{:S(2)}) async-start(), calls=%async_computation.4 | async-start | bytes 4194304 | tf_op jit(solution)/shard_map/psum | solution.py:12
  221.5 188.0 %reduce-scatter.5.cloned.1.call-start = ((), (), s32[]{:S(2)}) async-start(), calls=%async_computation.3 | async-start | bytes 1310720 | tf_op jit(solution)/shard_map/reduce_scatter | solution.py:48
Sparse Core Ops, SparseCore 0:
  20.5 153.7 all-reduce.6
  177.9 32.1 reduce-scatter.2
  221.6 152.0 all-reduce.4
  377.3 32.1 reduce-scatter.4
where the time goes:
time: 418 us; the launch traced here: 417 us
  waiting for transfers between devices  369 us (88%)
  blocking collectives  19.6 us (5%)
  between operations  14.5 us (3%)
  other arithmetic  7.75 us (2%)
    psum x2, waiting for transfers between devices, spread(): return lax.psum(jnp.where(mine, shard, jnp.zeros_like(shard)), axis)  306 us
    reduce_scatter x2, waiting for transfers between devices, local(): lax.psum_scatter(jnp.einsum('ik,qjk->qij', row_panel, grouped, preferred_...  62.7 us
    all_gather x2, blocking collectives, local(): row_panel = lax.all_gather(current, 'col', axis=1, tiled=True)  19.6 us
  transfers between devices with their start and end apart: 4, of which 4 were waited for; matrix products, arithmetic and copies ran while one was open for 0% of the time, Pallas kernels for 0%

commit v1 on v0

v1 whole, which is shorter than its diff:
```python
import functools

import jax
import jax.numpy as jnp
from jax import lax
from jax.experimental import pallas as pl
from jax.experimental.pallas import tpu as pltpu
from jax.sharding import PartitionSpec as P

BLOCK = 256
HALF = 128
STEPS = 2
MESH = pl.DeviceIdType.MESH
HALVES = ((0, HALF), (HALF, HALF))


def select_block(flag, values):
    kept = jnp.full(values.shape, flag, jnp.int32) == 1
    return jnp.where(kept, values, jnp.zeros_like(values))


def kernel(
    start_ref, square_ref, density_ref, out_ref,
    left_own, left_sib, right_own, right_sib, outgoing, incoming, swapped,
    z_send, z_recv, sib_send, sib_recv, far_send, far_recv, sum_send, sum_recv, swap_send, swap_recv,
):
    row, col, x = lax.axis_index("row"), lax.axis_index("col"), lax.axis_index("ka")
    yh, z = row // 8, lax.rem(row, 8)
    yl, core = col // 2, lax.rem(col, 2)

    def device(yh_, yl_, z_, core_, x_):
        return (yh_ * 8 + z_, yl_ * 2 + core_, x_)

    sibling = device(yh, yl, z, 1 - core, x)
    up = device(yh, yl, lax.rem(z + 1, 8), core, x)
    down = device(yh, yl, lax.rem(z + 7, 8), core, x)
    across = device(yl, yh, z, core, x)
    far = (device(1 - yh, yl, z, core, x), device(yh, 1 - yl, z, core, x))

    barrier = pltpu.get_barrier_semaphore()
    partners = [sibling, up, down, device(1 - yh, 1 - yl, z, core, x)]
    for dx in range(4):
        there = lax.rem(x + dx, 4)
        partners.append(device(1 - yh, yl, z, core, there))
        partners.append(device(yh, 1 - yl, z, core, there))
        if dx:
            partners.append(device(yh, yl, z, core, there))
    for partner in partners:
        pl.semaphore_signal(barrier, inc=1, device_id=partner, device_id_type=MESH)

    left_own[0, :BLOCK] = select_block(
        start_ref[row, col * 4 + x], density_ref[...]
    )
    pl.semaphore_wait(barrier, len(partners))

    def remote(src, dst, send, recv, target):
        return pltpu.make_async_remote_copy(
            src_ref=src, dst_ref=dst, send_sem=send, recv_sem=recv,
            device_id=target, device_id_type=MESH,
        )

    def ring_copy(step, slot, half):
        first, count = HALVES[half]
        downward = slot < 4 or (slot == 4 and half == 0)
        origin = slot - 1 if downward else (slot + 1) % 8
        here = pl.ds(first, count)
        src = left_own.at[step, here] if origin == 0 else right_own.at[step, origin, here]
        return remote(
            src, right_own.at[step, slot, here],
            z_send.at[step, slot, half], z_recv.at[step, slot, half],
            down if downward else up,
        )

    def sib_copy(step, slot, half):
        here = pl.ds(*HALVES[half])
        return remote(
            right_own.at[step, slot, here], right_sib.at[step, slot, here],
            sib_send.at[step, slot, half], sib_recv.at[step, slot, half], sibling,
        )

    def sib_left(step, part):
        here = pl.ds(part * BLOCK, BLOCK)
        return remote(
            left_own.at[step, here], left_sib.at[step, here],
            sib_send.at[step, 0, part], sib_recv.at[step, 0, part], sibling,
        )

    def far_copy(step):
        return remote(
            left_own.at[step, pl.ds(0, BLOCK)], left_own.at[step, pl.ds(BLOCK, BLOCK)],
            far_send.at[step], far_recv.at[step], far[step],
        )

    swap = remote(left_own.at[0, pl.ds(0, BLOCK)], swapped, swap_send, swap_recv, across)

    def owner(step, pair, part):
        x_ = lax.rem(z + pair, 4)
        if step == 0:
            y_ = yh if part == 0 else 1 - yh
            slot = jnp.where(y_ == yl, 0, 4) + lax.rem(x - x_ + 4, 4)
            return device(yh, y_, z, core, x_), slot
        y_ = yl if part == 0 else 1 - yl
        slot = jnp.where(y_ == yh, 0, 4) + lax.rem(x - x_ + 4, 4)
        return device(y_, yl, z, core, x_), slot

    def sum_copy(step, pair, part):
        target, slot = owner(step, pair, part)
        return remote(
            outgoing.at[step, pair, part], incoming.at[step, slot],
            sum_send.at[step, pair, part], sum_recv.at[step, slot], target,
        ), slot

    def multiply(step, slot):
        pair = slot % 4
        if slot:
            own, sib = right_own[step, slot], right_sib[step, slot]
        else:
            own, sib = left_own[step, :BLOCK], left_sib[step, :BLOCK]
        dims = (((1,), (1,)), ((), ()))
        product = lax.dot_general(left_own[step], own, dims, preferred_element_type=jnp.float32)
        product += lax.dot_general(left_sib[step], sib, dims, preferred_element_type=jnp.float32)
        product = product.astype(jnp.bfloat16)
        for part in range(2):
            outgoing[step, pair, part] = product[part * BLOCK:(part + 1) * BLOCK]
            copy, where = sum_copy(step, pair, part)

            @pl.when(where != 0)
            def _():
                copy.start()

    def consume(step, slot):
        @pl.when(lax.rem(z + slot, 8) // 4 == core)
        def _():
            multiply(step, slot)

    for step in range(STEPS):
        if step == 0:
            row_, block_ = yl * 8 + z, yh * 8 + core * 4 + x
        else:
            row_, block_ = row, col * 4 + x
        for slot, half in ((1, 0), (7, 1), (1, 1), (7, 0)):
            ring_copy(step, slot, half).start()
        far_copy(step).start()
        sib_left(step, 0).start()
        if step == 0:
            @pl.when(yh != yl)
            def _():
                swap.start()

            @pl.when(yh == yl)
            def _():
                swapped[...] = left_own[0, :BLOCK]

        for stage in range(1, 5):
            if stage < 4:
                arrivals = ((stage, 0), (8 - stage, 1), (stage, 1), (8 - stage, 0))
            else:
                arrivals = ((4, 0), (4, 1))
            for slot, half in arrivals:
                ring_copy(step, slot, half).wait_recv()
                if slot < 3 or (slot == 3 and half == 0):
                    ring_copy(step, slot + 1, half).start()
                if slot > 5 or (slot == 5 and half == 1):
                    ring_copy(step, slot - 1, half).start()
                sib_copy(step, slot, half).start()
            if stage == 1:
                far_copy(step).wait_recv()
                sib_left(step, 1).start()
                sib_left(step, 0).wait_recv()
                sib_left(step, 1).wait_recv()
                consume(step, 0)
            else:
                for slot in (stage - 1, 9 - stage):
                    for half in range(2):
                        sib_copy(step, slot, half).wait_recv()
                    consume(step, slot)
        for half in range(2):
            sib_copy(step, 4, half).wait_recv()
        consume(step, 4)

        mine = lax.rem(x - z + 8, 4)
        part_ = jnp.where(yh == yl, 0, 1)
        total = outgoing[step, mine, part_].astype(jnp.float32)
        for slot in range(1, 8):
            remote(
                outgoing.at[step, 0, 0], incoming.at[step, slot],
                sum_send.at[step, 0, 0], sum_recv.at[step, slot], sibling,
            ).wait_recv()
            total += incoming[step, slot].astype(jnp.float32)
        square = select_block(square_ref[row_, block_], total)
        if step == 0:
            @pl.when(yh != yl)
            def _():
                swap.wait_recv()

            following = 2.0 * swapped[...].astype(jnp.float32) - square
            left_own[1, :BLOCK] = following.astype(jnp.bfloat16)
        else:
            out_ref[...] = square.astype(jnp.bfloat16)

    for step in range(STEPS):
        for slot in range(1, 8):
            for half in range(2):
                ring_copy(step, slot, half).wait_send()
                sib_copy(step, slot, half).wait_send()
        far_copy(step).wait_send()
        for part in range(2):
            sib_left(step, part).wait_send()
        for pair in range(4):
            for part in range(2):
                copy, where = sum_copy(step, pair, part)

                @pl.when(where != 0)
                def _():
                    copy.wait_send()

    @pl.when(yh != yl)
    def _():
        swap.wait_send()


def local(density, pattern_start, pattern_square):
    block = (BLOCK, BLOCK)
    kind = jnp.bfloat16
    dma = pltpu.SemaphoreType.DMA
    return pl.pallas_call(
        kernel,
        name="purify",
        out_shape=jax.ShapeDtypeStruct(block, kind),
        in_specs=[
            pl.BlockSpec(memory_space=pltpu.SMEM),
            pl.BlockSpec(memory_space=pltpu.SMEM),
            pl.BlockSpec(memory_space=pltpu.VMEM),
        ],
        out_specs=pl.BlockSpec(memory_space=pltpu.VMEM),
        scratch_shapes=[
            pltpu.VMEM((STEPS, 2 * BLOCK, BLOCK), kind),
            pltpu.VMEM((STEPS, 2 * BLOCK, BLOCK), kind),
            pltpu.VMEM((STEPS, 8) + block, kind),
            pltpu.VMEM((STEPS, 8) + block, kind),
            pltpu.VMEM((STEPS, 4, 2) + block, kind),
            pltpu.VMEM((STEPS, 8) + block, kind),
            pltpu.VMEM(block, kind),
            dma((STEPS, 8, 2)), dma((STEPS, 8, 2)),
            dma((STEPS, 8, 2)), dma((STEPS, 8, 2)),
            dma((STEPS,)), dma((STEPS,)),
            dma((STEPS, 4, 2)), dma((STEPS, 8)),
            dma(()), dma(()),
        ],
        compiler_params=pltpu.CompilerParams(
            collective_id=0, has_side_effects=True, vmem_limit_bytes=40 * 2**20
        ),
    )(pattern_start, pattern_square, density)


def solution(mesh):
    return jax.shard_map(
        local,
        mesh=mesh,
        in_specs=(P("row", ("col", "ka")), P(), P()),
        out_specs=P("row", ("col", "ka")),
        check_vma=False,
    )
```

time: 418 us -> 65.7 us (0.16)
  waiting for transfers between devices: 369 us -> 0 us
  Pallas kernels: 0 us -> 62.6 us
  blocking collectives: 19.6 us -> 0 us
  between operations: 14.5 us -> 0.01 us
  other arithmetic: 7.75 us -> 0 us
    psum x2 -> x0, waiting for transfers between devices: 306 us -> none  [spread(): return lax.psum(jnp.where(mine, shard, jnp.zeros_like(shard)), axis)]
    reduce_scatter x2 -> x0, waiting for transfers between devices: 62.7 us -> none  [local(): lax.psum_scatter(jnp.einsum('ik,qjk->qij', row_panel, grouped, preferred_...]
    pallas_call x0 -> x1, Pallas kernels: none -> 62.6 us  [local(): pl.pallas_call(kernel, name='purify', out_shape=jax.ShapeDtypeStruct(bloc...]
    all_gather x2 -> x0, blocking collectives: 19.6 us -> none  [local(): row_panel = lax.all_gather(current, 'col', axis=1, tiled=True)]
  transfers between devices with their start and end apart: 4 -> 0, of which waited for: 4 -> 0; matrix products, arithmetic and copies ran while one was open for 0% -> 0% of each run, Pallas kernels for 0% -> 0%
where the time goes in v1:
time: 65.7 us; the launch traced here: 65.6 us
  Pallas kernels  62.6 us (95%)
  local copies, waits for them, and re-layouts  2.95 us (4%)
    pallas_call x1, Pallas kernels, local(): pl.pallas_call(kernel, name='purify', out_shape=jax.ShapeDtypeStruct(bloc...  62.6 us
    unnamed x7, local copies, waits for them, and re-layouts  2.95 us

profile of v1, /device:TPU:1, one launch (start us, length us, event | category | flops | bytes accessed | tf_op | source)
XLA Modules:
  0.0 65.6 jit_solution(4690441789230266493)
XLA Ops:
  0.0 0.0 copy-start
  0.0 0.9 %copy-done = bf16[256,256]{1,0:T(8,128)(2,1)S(1)} copy-done((bf16[256,256]{1,0:T(8,128)(2,1)S(1)}, bf16[256,256]{1,0:T(8,128)(2,1)}, u32[]{:S(2)}) %copy-start) | copy-done | bytes 131096
  0.9 0.0 copy-start.1
  0.9 0.7 %copy-done.1 = s32[16,16]{1,0:T(8,128)S(1)} copy-done((s32[16,16]{1,0:T(8,128)S(1)}, s32[16,16]{1,0:T(8,128)}, u32[]{:S(2)}) %copy-start.1) | copy-done | bytes 1048
  1.6 0.0 copy-start.2
  1.6 0.7 %copy-done.2 = s32[16,16]{1,0:T(8,128)S(1)} copy-done((s32[16,16]{1,0:T(8,128)S(1)}, s32[16,16]{1,0:T(8,128)}, u32[]{:S(2)}) %copy-start.2) | copy-done | bytes 1048
  2.3 62.6 %purify.1 = bf16[256,256]{1,0:T(8,128)(2,1)S(1)} custom-call(s32[16,16]{1,0:T(8,128)S(1)} %copy-done.1, s32[16,16]{1,0:T(8,128)S(1)} %copy-done.2, bf16[256,256]{1,0:T(8,128)(2,1)S(1)} %copy-done), custom_call_target="tpu_custom_call" | custom-call | tf_op jit(solution)/shard_map/purify/pallas_call | solution.py:226
  64.9 0.7 %copy.5 = bf16[256,256]{1,0:T(8,128)(2,1)} copy(bf16[256,256]{1,0:T(8,128)(2,1)S(1)} %purify.1) | data formatting | bytes 262144
Async XLA Ops:
  0.0 0.9 %copy-start = (bf16[256,256]{1,0:T(8,128)(2,1)S(1)}, bf16[256,256]{1,0:T(8,128)(2,1)}, u32[]{:S(2)}) copy-start(bf16[256,256]{1,0:T(8,128)(2,1)} %density_ref.1) | copy-start | bytes 393220
  0.9 0.7 %copy-start.1 = (s32[16,16]{1,0:T(8,128)S(1)}, s32[16,16]{1,0:T(8,128)}, u32[]{:S(2)}) copy-start(s32[16,16]{1,0:T(8,128)} %start_ref.1) | copy-start | bytes 3076
  1.6 0.7 %copy-start.2 = (s32[16,16]{1,0:T(8,128)S(1)}, s32[16,16]{1,0:T(8,128)}, u32[]{:S(2)}) copy-start(s32[16,16]{1,0:T(8,128)} %square_ref.1) | copy-start | bytes 3076

commit v2 on v1

--- a/solution.py
+++ b/solution.py
@@ -8,10 +8,11 @@
 from jax.sharding import PartitionSpec as P
 
 BLOCK = 256
-HALF = 128
+CHUNKS = 4
+CHUNK = BLOCK // CHUNKS
+HALF = BLOCK // 2
 STEPS = 2
 MESH = pl.DeviceIdType.MESH
-HALVES = ((0, HALF), (HALF, HALF))
 
 
 def select_block(flag, values):
@@ -19,9 +20,19 @@
     return jnp.where(kept, values, jnp.zeros_like(values))
 
 
+def order(stage):
+    near = range(CHUNKS // 2)
+    rest = range(CHUNKS // 2, CHUNKS)
+    if stage == 4:
+        pairs = [((4, c), (4, c + CHUNKS // 2)) for c in near]
+    else:
+        pairs = [((stage, c), (8 - stage, d)) for c, d in zip([*near, *rest], [*rest, *near])]
+    return [item for pair in pairs for item in pair]
+
+
 def kernel(
-    start_ref, square_ref, density_ref, out_ref,
-    left_own, left_sib, right_own, right_sib, outgoing, incoming, swapped,
+    start_hbm, square_hbm, density_hbm, out_ref,
+    density_ref, start_ref, square_ref, load_sem, left_own, left_sib, right_own, right_sib, outgoing, incoming, swapped,
     z_send, z_recv, sib_send, sib_recv, far_send, far_recv, sum_send, sum_recv, swap_send, swap_recv,
 ):
     row, col, x = lax.axis_index("row"), lax.axis_index("col"), lax.axis_index("ka")
@@ -36,6 +47,15 @@
     down = device(yh, yl, lax.rem(z + 7, 8), core, x)
     across = device(yl, yh, z, core, x)
     far = (device(1 - yh, yl, z, core, x), device(yh, 1 - yl, z, core, x))
+
+    loads = [
+        pltpu.make_async_copy(src, dst, load_sem.at[i])
+        for i, (src, dst) in enumerate(
+            ((density_hbm, density_ref), (start_hbm, start_ref), (square_hbm, square_ref))
+        )
+    ]
+    for load in loads:
+        load.start()
 
     barrier = pltpu.get_barrier_semaphore()
     partners = [sibling, up, down, device(1 - yh, 1 - yl, z, core, x)]
@@ -48,6 +68,8 @@
     for partner in partners:
         pl.semaphore_signal(barrier, inc=1, device_id=partner, device_id_type=MESH)
 
+    for load in loads:
+        load.wait()
     left_own[0, :BLOCK] = select_block(
         start_ref[row, col * 4 + x], density_ref[...]
     )
@@ -59,20 +81,19 @@
             device_id=target, device_id_type=MESH,
         )
 
-    def ring_copy(step, slot, half):
-        first, count = HALVES[half]
-        downward = slot < 4 or (slot == 4 and half == 0)
+    def ring_copy(step, slot, chunk):
+        downward = slot < 4 or (slot == 4 and chunk < CHUNKS // 2)
         origin = slot - 1 if downward else (slot + 1) % 8
-        here = pl.ds(first, count)
+        here = pl.ds(chunk * CHUNK, CHUNK)
         src = left_own.at[step, here] if origin == 0 else right_own.at[step, origin, here]
         return remote(
             src, right_own.at[step, slot, here],
-            z_send.at[step, slot, half], z_recv.at[step, slot, half],
+            z_send.at[step, slot, chunk], z_recv.at[step, slot, chunk],
             down if downward else up,
         )
 
     def sib_copy(step, slot, half):
-        here = pl.ds(*HALVES[half])
+        here = pl.ds(half * HALF, HALF)
         return remote(
             right_own.at[step, slot, here], right_sib.at[step, slot, here],
             sib_send.at[step, slot, half], sib_recv.at[step, slot, half], sibling,
@@ -138,8 +159,8 @@
             row_, block_ = yl * 8 + z, yh * 8 + core * 4 + x
         else:
             row_, block_ = row, col * 4 + x
-        for slot, half in ((1, 0), (7, 1), (1, 1), (7, 0)):
-            ring_copy(step, slot, half).start()
+        for slot, chunk in order(1):
+            ring_copy(step, slot, chunk).start()
         far_copy(step).start()
         sib_left(step, 0).start()
         if step == 0:
@@ -152,31 +173,22 @@
                 swapped[...] = left_own[0, :BLOCK]
 
         for stage in range(1, 5):
-            if stage < 4:
-                arrivals = ((stage, 0), (8 - stage, 1), (stage, 1), (8 - stage, 0))
-            else:
-                arrivals = ((4, 0), (4, 1))
-            for slot, half in arrivals:
-                ring_copy(step, slot, half).wait_recv()
-                if slot < 3 or (slot == 3 and half == 0):
-                    ring_copy(step, slot + 1, half).start()
-                if slot > 5 or (slot == 5 and half == 1):
-                    ring_copy(step, slot - 1, half).start()
-                sib_copy(step, slot, half).start()
+            for slot, chunk in order(stage):
+                ring_copy(step, slot, chunk).wait_recv()
+                if stage < 3 or (stage == 3 and (slot == 3) == (chunk < CHUNKS // 2)):
+                    ring_copy(step, slot + 1 if slot < 4 else slot - 1, chunk).start()
+                if chunk % (CHUNKS // 2) == CHUNKS // 2 - 1:
+                    sib_copy(step, slot, chunk // (CHUNKS // 2)).start()
             if stage == 1:
                 far_copy(step).wait_recv()
                 sib_left(step, 1).start()
                 sib_left(step, 0).wait_recv()
                 sib_left(step, 1).wait_recv()
                 consume(step, 0)
-            else:
-                for slot in (stage - 1, 9 - stage):
-                    for half in range(2):
-                        sib_copy(step, slot, half).wait_recv()
-                    consume(step, slot)
-        for half in range(2):
-            sib_copy(step, 4, half).wait_recv()
-        consume(step, 4)
+            for slot in (stage, 8 - stage) if stage < 4 else (4,):
+                for half in range(2):
+                    sib_copy(step, slot, half).wait_recv()
+                consume(step, slot)
 
         mine = lax.rem(x - z + 8, 4)
         part_ = jnp.where(yh == yl, 0, 1)
@@ -200,8 +212,9 @@
 
     for step in range(STEPS):
         for slot in range(1, 8):
+            for chunk in range(CHUNKS):
+                ring_copy(step, slot, chunk).wait_send()
             for half in range(2):
-                ring_copy(step, slot, half).wait_send()
                 sib_copy(step, slot, half).wait_send()
         far_copy(step).wait_send()
         for part in range(2):
@@ -228,12 +241,16 @@
         name="purify",
         out_shape=jax.ShapeDtypeStruct(block, kind),
         in_specs=[
-            pl.BlockSpec(memory_space=pltpu.SMEM),
-            pl.BlockSpec(memory_space=pltpu.SMEM),
-            pl.BlockSpec(memory_space=pltpu.VMEM),
+            pl.BlockSpec(memory_space=pl.ANY),
+            pl.BlockSpec(memory_space=pl.ANY),
+            pl.BlockSpec(memory_space=pl.ANY),
         ],
         out_specs=pl.BlockSpec(memory_space=pltpu.VMEM),
         scratch_shapes=[
+            pltpu.VMEM(block, kind),
+            pltpu.SMEM(pattern_start.shape, jnp.int32),
+            pltpu.SMEM(pattern_square.shape, jnp.int32),
+            dma((3,)),
             pltpu.VMEM((STEPS, 2 * BLOCK, BLOCK), kind),
             pltpu.VMEM((STEPS, 2 * BLOCK, BLOCK), kind),
             pltpu.VMEM((STEPS, 8) + block, kind),
@@ -241,14 +258,14 @@
             pltpu.VMEM((STEPS, 4, 2) + block, kind),
             pltpu.VMEM((STEPS, 8) + block, kind),
             pltpu.VMEM(block, kind),
-            dma((STEPS, 8, 2)), dma((STEPS, 8, 2)),
+            dma((STEPS, 8, CHUNKS)), dma((STEPS, 8, CHUNKS)),
             dma((STEPS, 8, 2)), dma((STEPS, 8, 2)),
             dma((STEPS,)), dma((STEPS,)),
             dma((STEPS, 4, 2)), dma((STEPS, 8)),
             dma(()), dma(()),
         ],
         compiler_params=pltpu.CompilerParams(
-            collective_id=0, has_side_effects=True, vmem_limit_bytes=40 * 2**20
+            collective_id=0, has_side_effects=True, vmem_limit_bytes=62 * 2**20
         ),
     )(pattern_start, pattern_square, density)
 

time: 65.7 us -> 62.9 us (0.957)
  Pallas kernels: 62.6 us -> 61.1 us
  local copies, waits for them, and re-layouts: 2.95 us -> 1.57 us
    pallas_call x1, Pallas kernels: 62.6 us -> 61.1 us  [local(): pl.pallas_call(kernel, name='purify', out_shape=jax.ShapeDtypeStruct(bloc...]
    unnamed x7 -> x1, local copies, waits for them, and re-layouts: 2.95 us -> 1.57 us
where the time goes in v2:
time: 62.9 us; the launch traced here: 62.7 us
  Pallas kernels  61.1 us (97%)
  local copies, waits for them, and re-layouts  1.57 us (2%)
    pallas_call x1, Pallas kernels, local(): pl.pallas_call(kernel, name='purify', out_shape=jax.ShapeDtypeStruct(bloc...  61.1 us
    unnamed x1, local copies, waits for them, and re-layouts  1.57 us

profile of v2, /device:TPU:1, one launch (start us, length us, event | category | flops | bytes accessed | tf_op | source)
XLA Modules:
  0.0 62.7 jit_solution(5838728897117732743)
XLA Ops:
  0.0 61.1 %purify.1 = bf16[256,256]{1,0:T(8,128)(2,1)} custom-call(s32[16,16]{1,0:T(8,128)} %start_hbm.1, s32[16,16]{1,0:T(8,128)} %square_hbm.1, bf16[256,256]{1,0:T(8,128)(2,1)} %density_hbm.1), custom_call_target="tpu_custom_call" | custom-call | tf_op jit(solution)/shard_map/purify/pallas_call | solution.py:239
  61.2 1.6 %copy.5 = bf16[256,256]{1,0:T(8,128)(2,1)} copy(bf16[256,256]{1,0:T(8,128)(2,1)} %purify.1) | data formatting | bytes 262144

commit v3 on v2

v3 whole, which is shorter than its diff:
```python
import jax
import jax.numpy as jnp
from jax import lax
from jax.experimental import pallas as pl
from jax.experimental.pallas import tpu as pltpu
from jax.sharding import PartitionSpec as P

BLOCK = 256
HALF = BLOCK // 2
STEPS = 2
MESH = pl.DeviceIdType.MESH


def select_block(flag, values):
    kept = jnp.full(values.shape, flag, jnp.int32) == 1
    return jnp.where(kept, values, jnp.zeros_like(values))


def order(stage):
    if stage == 4:
        return ((4, 0), (4, 1))
    return ((stage, 0), (8 - stage, 1), (stage, 1), (8 - stage, 0))


def kernel(
    start_hbm, square_hbm, density_hbm, out_ref,
    density_ref, start_ref, square_ref, load_sem, left, right, outgoing, incoming, swapped,
    z_send, z_recv, sib_send, sib_recv, far_send, far_recv, sum_send, sum_recv, swap_send, swap_recv,
):
    row, col, x = lax.axis_index("row"), lax.axis_index("col"), lax.axis_index("ka")
    yh, z = row // 8, lax.rem(row, 8)
    yl, core = col // 2, lax.rem(col, 2)

    def device(yh_, yl_, z_, core_, x_):
        return (yh_ * 8 + z_, yl_ * 2 + core_, x_)

    above, below = lax.rem(z + 1, 8), lax.rem(z + 7, 8)
    sibling = device(yh, yl, z, 1 - core, x)
    across = device(yl, yh, z, core, x)

    def over_yh(step):
        return yh + (1 - step) * (1 - 2 * yh)

    def over_yl(step):
        return yl + step * (1 - 2 * yl)

    loads = [
        pltpu.make_async_copy(src, dst, load_sem.at[i])
        for i, (src, dst) in enumerate(
            ((density_hbm, density_ref), (start_hbm, start_ref), (square_hbm, square_ref))
        )
    ]
    for load in loads:
        load.start()

    barrier = pltpu.get_barrier_semaphore()
    partners = [sibling, device(1 - yh, 1 - yl, z, core, x)]
    for z_ in (above, below):
        partners += [device(yh, yl, z_, core, x), device(yh, yl, z_, 1 - core, x)]
    for dx in range(4):
        there = lax.rem(x + dx, 4)
        partners.append(device(1 - yh, yl, z, core, there))
        partners.append(device(yh, 1 - yl, z, core, there))
        if dx:
            partners.append(device(yh, yl, z, core, there))
    for partner in partners:
        pl.semaphore_signal(barrier, inc=1, device_id=partner, device_id_type=MESH)

    for load in loads:
        load.wait()
    left[0, 0, :BLOCK] = select_block(start_ref[row, col * 4 + x], density_ref[...])
    pl.semaphore_wait(barrier, len(partners))

    def remote(src, dst, send, recv, target):
        return pltpu.make_async_remote_copy(
            src_ref=src, dst_ref=dst, send_sem=send, recv_sem=recv,
            device_id=target, device_id_type=MESH,
        )

    def user(z_, slot):
        return lax.rem(z_ + slot, 8) // 4

    def rows(half):
        return pl.ds(half * HALF, HALF)

    def ring_copy(step, slot, half):
        downward = slot < 4 or (slot == 4 and half == 0)
        origin = slot - 1 if downward else (slot + 1) % 8
        z_ = below if downward else above
        core_ = user(z_, 4) if slot == 4 else core
        lane = jnp.where(core_ == core, 0, 1) if slot == 4 else 0
        src = left.at[step, 0, rows(half)] if origin == 0 else right.at[step, 0, origin, rows(half)]
        return remote(
            src, right.at[step, lane, slot, rows(half)],
            z_send.at[step, slot, half], z_recv.at[step, lane, slot, half],
            device(yh, yl, z_, core_, x),
        )

    def ring_arrival(step, lane, slot, half):
        here = right.at[step, lane, slot, rows(half)]
        return remote(here, here, z_send.at[step, slot, half], z_recv.at[step, lane, slot, half], sibling)

    def sib_copy(step, slot, half):
        return remote(
            right.at[step, 0, slot, rows(half)], right.at[step, 1, slot, rows(half)],
            sib_send.at[step, slot, half], sib_recv.at[step, slot, half], sibling,
        )

    def sib_left(step, part):
        here = pl.ds(part * BLOCK, BLOCK)
        return remote(
            left.at[step, 0, here], left.at[step, 1, here],
            sib_send.at[step, 0, part], sib_recv.at[step, 0, part], sibling,
        )

    def far_copy(step):
        return remote(
            left.at[step, 0, pl.ds(0, BLOCK)], left.at[step, 0, pl.ds(BLOCK, BLOCK)],
            far_send.at[step], far_recv.at[step],
            device(over_yh(step), over_yl(step), z, core, x),
        )

    swap = remote(left.at[0, 0, pl.ds(0, BLOCK)], swapped, swap_send, swap_recv, across)

    def sum_copy(step, pair, crossing, half):
        x_ = lax.rem(z + pair, 4)
        slot = 4 * crossing + lax.rem(x - x_ + 4, 4)
        target = device(
            jnp.where(crossing != 0, over_yh(1 - step), yh),
            jnp.where(crossing != 0, over_yl(1 - step), yl), z, core, x_,
        )
        return remote(
            outgoing.at[step, pair, crossing, rows(half)], incoming.at[step, slot, rows(half)],
            sum_send.at[step, pair, crossing, half], sum_recv.at[step, slot, half], target,
        )

    def elsewhere(pair):
        return lax.rem(z + pair, 4) != x

    def multiply_part(step, slot, part):
        pair = slot % 4
        crossing = jnp.where(yh == yl, part, 1 - part)
        dims = (((1,), (1,)), ((), ()))
        here = pl.ds(part * BLOCK, BLOCK)
        product = jnp.zeros((BLOCK, BLOCK), jnp.float32)
        for lane in range(2):
            other = right[step, lane, slot] if slot else left[step, lane, :BLOCK]
            product += lax.dot_general(
                left[step, lane, here], other, dims, preferred_element_type=jnp.float32
            )
        outgoing[step, pair, crossing] = product.astype(jnp.bfloat16)

        @pl.when(jnp.logical_or(crossing != 0, elsewhere(pair)))
        def _():
            for half in range(2):
                sum_copy(step, pair, crossing, half).start()

    def multiply(step, slot):
        @pl.when(yh == yl)
        def _():
            for part in (1, 0):
                multiply_part(step, slot, part)

        @pl.when(yh != yl)
        def _():
            for part in (0, 1):
                multiply_part(step, slot, part)

    for slot, half in order(1):
        ring_copy(0, slot, half).start()

    @pl.when(yh != yl)
    def _():
        swap.start()

    @pl.when(yh == yl)
    def _():
        swapped[...] = left[0, 0, :BLOCK]

    @pl.loop(0, STEPS)
    def _(step):
        row_ = jnp.where(step == 0, yl, yh) * 8 + z
        block_ = jnp.where(step == 0, yh, yl) * 8 + core * 4 + x
        far_copy(step).start()
        sib_left(step, 0).start()
        for stage in range(1, 4):
            for slot, half in order(stage):
                ring_copy(step, slot, half).wait_recv()
                if stage < 3 or (slot == 3) == (half == 0):
                    ring_copy(step, slot + 1 if slot < 4 else slot - 1, half).start()

                @pl.when(user(z, slot) != core)
                def _():
                    sib_copy(step, slot, half).start()
            if stage == 1:
                far_copy(step).wait_recv()
                sib_left(step, 1).start()
                sib_left(step, 0).wait_recv()

                @pl.when(user(z, 0) == core)
                def _():
                    multiply_part(step, 0, 0)

                for slot in (1, 7):
                    @pl.when(user(z, slot) == core)
                    def _():
                        for half in range(2):
                            sib_copy(step, slot, half).wait_recv()
                        multiply_part(step, slot, 0)

                sib_left(step, 1).wait_recv()
                for slot in (0, 1, 7):
                    @pl.when(user(z, slot) == core)
                    def _():
                        multiply_part(step, slot, 1)
            else:
                for slot in (stage, 8 - stage):
                    @pl.when(user(z, slot) == core)
                    def _():
                        for half in range(2):
                            sib_copy(step, slot, half).wait_recv()
                        multiply(step, slot)

        @pl.when(user(z, 4) == core)
        def _():
            for lane in range(2):
                for half in range(2):
                    ring_arrival(step, lane, 4, half).wait_recv()
            multiply(step, 4)

        @pl.when(jnp.logical_and(step == 0, yh != yl))
        def _():
            swap.wait_recv()

        mine = lax.rem(x - z + 8, 4)
        for half in range(2):
            total = outgoing[step, mine, 0, rows(half)].astype(jnp.float32)
            for slot in range(1, 8):
                here = incoming.at[step, slot, rows(half)]
                remote(
                    here, here, sum_send.at[step, 0, 0, half], sum_recv.at[step, slot, half], sibling
                ).wait_recv()
                total += incoming[step, slot, rows(half)].astype(jnp.float32)
            square = select_block(square_ref[row_, block_], total)

            @pl.when(step == 0)
            def _():
                following = 2.0 * swapped[rows(half)].astype(jnp.float32) - square
                left[1, 0, rows(half)] = following.astype(jnp.bfloat16)
                for slot in (1, 7):
                    ring_copy(1, slot, half).start()

            @pl.when(step != 0)
            def _():
                out_ref[rows(half)] = square.astype(jnp.bfloat16)

    @pl.loop(0, STEPS)
    def _(step):
        for slot in range(1, 8):
            for half in range(2):
                ring_copy(step, slot, half).wait_send()
                if slot != 4:
                    @pl.when(user(z, slot) != core)
                    def _():
                        sib_copy(step, slot, half).wait_send()
        far_copy(step).wait_send()
        for part in range(2):
            sib_left(step, part).wait_send()
        for pair in range(4):
            for half in range(2):
                sum_copy(step, pair, 1, half).wait_send()

                @pl.when(elsewhere(pair))
                def _():
                    sum_copy(step, pair, 0, half).wait_send()

    @pl.when(yh != yl)
    def _():
        swap.wait_send()


def local(density, pattern_start, pattern_square):
    block = (BLOCK, BLOCK)
    kind = jnp.bfloat16
    dma = pltpu.SemaphoreType.DMA
    return pl.pallas_call(
        kernel,
        name="purify",
        out_shape=jax.ShapeDtypeStruct(block, kind),
        in_specs=[pl.BlockSpec(memory_space=pl.ANY)] * 3,
        out_specs=pl.BlockSpec(memory_space=pltpu.VMEM),
        scratch_shapes=[
            pltpu.VMEM(block, kind),
            pltpu.SMEM(pattern_start.shape, jnp.int32),
            pltpu.SMEM(pattern_square.shape, jnp.int32),
            dma((3,)),
            pltpu.VMEM((STEPS, 2, 2 * BLOCK, BLOCK), kind),
            pltpu.VMEM((STEPS, 2, 8) + block, kind),
            pltpu.VMEM((STEPS, 4, 2) + block, kind),
            pltpu.VMEM((STEPS, 8) + block, kind),
            pltpu.VMEM(block, kind),
            dma((STEPS, 8, 2)), dma((STEPS, 2, 8, 2)),
            dma((STEPS, 8, 2)), dma((STEPS, 8, 2)),
            dma((STEPS,)), dma((STEPS,)),
            dma((STEPS, 4, 2, 2)), dma((STEPS, 8, 2)),
            dma(()), dma(()),
        ],
        compiler_params=pltpu.CompilerParams(
            collective_id=0, has_side_effects=True, vmem_limit_bytes=62 * 2**20
        ),
    )(pattern_start, pattern_square, density)


def solution(mesh):
    return jax.shard_map(
        local,
        mesh=mesh,
        in_specs=(P("row", ("col", "ka")), P(), P()),
        out_specs=P("row", ("col", "ka")),
        check_vma=False,
    )
```

time: 62.9 us -> 61.5 us (0.978)
  Pallas kernels: 61.1 us -> 59.8 us
    pallas_call x1, Pallas kernels: 61.1 us -> 59.8 us  [local(): pl.pallas_call(kernel, name='purify', out_shape=jax.ShapeDtypeStruct(bloc...]
where the time goes in v3:
time: 61.5 us; the launch traced here: 61.4 us
  Pallas kernels  59.8 us (97%)
  local copies, waits for them, and re-layouts  1.57 us (3%)
    pallas_call x1, Pallas kernels, local(): pl.pallas_call(kernel, name='purify', out_shape=jax.ShapeDtypeStruct(bloc...  59.8 us
    unnamed x1, local copies, waits for them, and re-layouts  1.57 us

profile of v3, /device:TPU:1, one launch (start us, length us, event | category | flops | bytes accessed | tf_op | source)
XLA Modules:
  0.0 61.4 jit_solution(13626845476740976633)
XLA Ops:
  0.0 59.8 %purify.1 = bf16[256,256]{1,0:T(8,128)(2,1)} custom-call(s32[16,16]{1,0:T(8,128)} %start_hbm.1, s32[16,16]{1,0:T(8,128)} %square_hbm.1, bf16[256,256]{1,0:T(8,128)(2,1)} %density_hbm.1), custom_call_target="tpu_custom_call" | custom-call | tf_op jit(solution)/shard_map/purify/pallas_call | solution.py:286
  59.8 1.6 %copy.5 = bf16[256,256]{1,0:T(8,128)(2,1)} copy(bf16[256,256]{1,0:T(8,128)(2,1)} %purify.1) | data formatting | bytes 262144

commit v4 on v3

--- a/solution.py
+++ b/solution.py
@@ -25,7 +25,7 @@
 def kernel(
     start_hbm, square_hbm, density_hbm, out_ref,
     density_ref, start_ref, square_ref, load_sem, left, right, outgoing, incoming, swapped,
-    z_send, z_recv, sib_send, sib_recv, far_send, far_recv, sum_send, sum_recv, swap_send, swap_recv,
+    z_send, z_recv, sib_send, sib_recv, far_send, far_recv, sum_send, sum_recv, swap_send, swap_recv, ready, out_sem, out_block,
 ):
     row, col, x = lax.axis_index("row"), lax.axis_index("col"), lax.axis_index("ka")
     yh, z = row // 8, lax.rem(row, 8)
@@ -57,12 +57,12 @@
     partners = [sibling, device(1 - yh, 1 - yl, z, core, x)]
     for z_ in (above, below):
         partners += [device(yh, yl, z_, core, x), device(yh, yl, z_, 1 - core, x)]
-    for dx in range(4):
-        there = lax.rem(x + dx, 4)
-        partners.append(device(1 - yh, yl, z, core, there))
-        partners.append(device(yh, 1 - yl, z, core, there))
-        if dx:
-            partners.append(device(yh, yl, z, core, there))
+    beside = (device(yh, 1 - yl, z, core, x), device(1 - yh, yl, z, core, x))
+    partners += beside
+    for dx in (1, 2, 3):
+        partners.append(device(yh, yl, z, core, lax.rem(x + dx, 4)))
+    for dx in (1, 3):
+        partners.append(device(yh, 1 - yl, z, core, lax.rem(x + dx, 4)))
     for partner in partners:
         pl.semaphore_signal(barrier, inc=1, device_id=partner, device_id_type=MESH)
 
@@ -70,6 +70,8 @@
         load.wait()
     left[0, 0, :BLOCK] = select_block(start_ref[row, col * 4 + x], density_ref[...])
     pl.semaphore_wait(barrier, len(partners))
+    for neighbour in beside:
+        pl.semaphore_signal(ready, inc=1, device_id=neighbour, device_id_type=MESH)
 
     def remote(src, dst, send, recv, target):
         return pltpu.make_async_remote_copy(
@@ -133,6 +135,9 @@
             outgoing.at[step, pair, crossing, rows(half)], incoming.at[step, slot, rows(half)],
             sum_send.at[step, pair, crossing, half], sum_recv.at[step, slot, half], target,
         )
+
+    def out_copy(half):
+        return pltpu.make_async_copy(out_block.at[rows(half)], out_ref.at[rows(half)], out_sem.at[half])
 
     def elsewhere(pair):
         return lax.rem(z + pair, 4) != x
@@ -197,6 +202,10 @@
                 sib_left(step, 1).start()
                 sib_left(step, 0).wait_recv()
 
+                @pl.when(step == 0)
+                def _():
+                    pl.semaphore_wait(ready, len(beside))
+
                 @pl.when(user(z, 0) == core)
                 def _():
                     multiply_part(step, 0, 0)
@@ -252,7 +261,8 @@
 
             @pl.when(step != 0)
             def _():
-                out_ref[rows(half)] = square.astype(jnp.bfloat16)
+                out_block[rows(half)] = square.astype(jnp.bfloat16)
+                out_copy(half).start()
 
     @pl.loop(0, STEPS)
     def _(step):
@@ -278,6 +288,9 @@
     def _():
         swap.wait_send()
 
+    for half in range(2):
+        out_copy(half).wait()
+
 
 def local(density, pattern_start, pattern_square):
     block = (BLOCK, BLOCK)
@@ -288,7 +301,7 @@
         name="purify",
         out_shape=jax.ShapeDtypeStruct(block, kind),
         in_specs=[pl.BlockSpec(memory_space=pl.ANY)] * 3,
-        out_specs=pl.BlockSpec(memory_space=pltpu.VMEM),
+        out_specs=pl.BlockSpec(memory_space=pl.ANY),
         scratch_shapes=[
             pltpu.VMEM(block, kind),
             pltpu.SMEM(pattern_start.shape, jnp.int32),
@@ -304,6 +317,7 @@
             dma((STEPS,)), dma((STEPS,)),
             dma((STEPS, 4, 2, 2)), dma((STEPS, 8, 2)),
             dma(()), dma(()),
+            pltpu.SemaphoreType.REGULAR, dma((2,)), pltpu.VMEM(block, kind),
         ],
         compiler_params=pltpu.CompilerParams(
             collective_id=0, has_side_effects=True, vmem_limit_bytes=62 * 2**20

time: 61.5 us -> 61 us (level)
  no operation moved by 1% of the time
where the time goes in v4:
time: 61 us; the launch traced here: 60.9 us
  Pallas kernels  59.3 us (97%)
  local copies, waits for them, and re-layouts  1.57 us (3%)
    pallas_call x1, Pallas kernels, local(): pl.pallas_call(kernel, name='purify', out_shape=jax.ShapeDtypeStruct(bloc...  59.3 us
    unnamed x1, local copies, waits for them, and re-layouts  1.57 us

profile of v4, /device:TPU:1, one launch (start us, length us, event | category | flops | bytes accessed | tf_op | source)
XLA Modules:
  0.0 60.9 jit_solution(10834982930383433615)
XLA Ops:
  0.0 59.3 %purify.1 = bf16[256,256]{1,0:T(8,128)(2,1)} custom-call(s32[16,16]{1,0:T(8,128)} %start_hbm.1, s32[16,16]{1,0:T(8,128)} %square_hbm.1, bf16[256,256]{1,0:T(8,128)(2,1)} %density_hbm.1), custom_call_target="tpu_custom_call" | custom-call | tf_op jit(solution)/shard_map/purify/pallas_call | solution.py:299
  59.3 1.6 %copy.5 = bf16[256,256]{1,0:T(8,128)(2,1)} copy(bf16[256,256]{1,0:T(8,128)(2,1)} %purify.1) | data formatting | bytes 262144

commit v5 on v4

--- a/solution.py
+++ b/solution.py
@@ -66,12 +66,10 @@
     for partner in partners:
         pl.semaphore_signal(barrier, inc=1, device_id=partner, device_id_type=MESH)
 
-    for load in loads:
+    for load in loads[:2]:
         load.wait()
     left[0, 0, :BLOCK] = select_block(start_ref[row, col * 4 + x], density_ref[...])
     pl.semaphore_wait(barrier, len(partners))
-    for neighbour in beside:
-        pl.semaphore_signal(ready, inc=1, device_id=neighbour, device_id_type=MESH)
 
     def remote(src, dst, send, recv, target):
         return pltpu.make_async_remote_copy(
@@ -102,10 +100,10 @@
         here = right.at[step, lane, slot, rows(half)]
         return remote(here, here, z_send.at[step, slot, half], z_recv.at[step, lane, slot, half], sibling)
 
-    def sib_copy(step, slot, half):
-        return remote(
-            right.at[step, 0, slot, rows(half)], right.at[step, 1, slot, rows(half)],
-            sib_send.at[step, slot, half], sib_recv.at[step, slot, half], sibling,
+    def sib_copy(step, slot):
+        return remote(
+            right.at[step, 0, slot], right.at[step, 1, slot],
+            sib_send.at[step, slot, 0], sib_recv.at[step, slot, 0], sibling,
         )
 
     def sib_left(step, part):
@@ -173,6 +171,9 @@
 
     for slot, half in order(1):
         ring_copy(0, slot, half).start()
+    for neighbour in beside:
+        pl.semaphore_signal(ready, inc=1, device_id=neighbour, device_id_type=MESH)
+    loads[2].wait()
 
     @pl.when(yh != yl)
     def _():
@@ -194,9 +195,10 @@
                 if stage < 3 or (slot == 3) == (half == 0):
                     ring_copy(step, slot + 1 if slot < 4 else slot - 1, half).start()
 
-                @pl.when(user(z, slot) != core)
-                def _():
-                    sib_copy(step, slot, half).start()
+                if (slot < 4) == (half == 1):
+                    @pl.when(user(z, slot) != core)
+                    def _():
+                        sib_copy(step, slot).start()
             if stage == 1:
                 far_copy(step).wait_recv()
                 sib_left(step, 1).start()
@@ -213,8 +215,7 @@
                 for slot in (1, 7):
                     @pl.when(user(z, slot) == core)
                     def _():
-                        for half in range(2):
-                            sib_copy(step, slot, half).wait_recv()
+                        sib_copy(step, slot).wait_recv()
                         multiply_part(step, slot, 0)
 
                 sib_left(step, 1).wait_recv()
@@ -226,8 +227,7 @@
                 for slot in (stage, 8 - stage):
                     @pl.when(user(z, slot) == core)
                     def _():
-                        for half in range(2):
-                            sib_copy(step, slot, half).wait_recv()
+                        sib_copy(step, slot).wait_recv()
                         multiply(step, slot)
 
         @pl.when(user(z, 4) == core)
@@ -269,10 +269,10 @@
         for slot in range(1, 8):
             for half in range(2):
                 ring_copy(step, slot, half).wait_send()
-                if slot != 4:
+                if slot != 4 and half == 0:
                     @pl.when(user(z, slot) != core)
                     def _():
-                        sib_copy(step, slot, half).wait_send()
+                        sib_copy(step, slot).wait_send()
         far_copy(step).wait_send()
         for part in range(2):
             sib_left(step, part).wait_send()

time: 61 us -> 61.1 us (level)
  no operation moved by 1% of the time
where the time goes in v5:
time: 61.1 us; the launch traced here: 60.9 us
  Pallas kernels  59.4 us (97%)
  local copies, waits for them, and re-layouts  1.57 us (3%)
    pallas_call x1, Pallas kernels, local(): pl.pallas_call(kernel, name='purify', out_shape=jax.ShapeDtypeStruct(bloc...  59.4 us
    unnamed x1, local copies, waits for them, and re-layouts  1.57 us

profile of v5, /device:TPU:1, one launch (start us, length us, event | category | flops | bytes accessed | tf_op | source)
XLA Modules:
  0.0 60.9 jit_solution(12159227444906955679)
XLA Ops:
  0.0 59.4 %purify.1 = bf16[256,256]{1,0:T(8,128)(2,1)} custom-call(s32[16,16]{1,0:T(8,128)} %start_hbm.1, s32[16,16]{1,0:T(8,128)} %square_hbm.1, bf16[256,256]{1,0:T(8,128)(2,1)} %density_hbm.1), custom_call_target="tpu_custom_call" | custom-call | tf_op jit(solution)/shard_map/purify/pallas_call | solution.py:299
  59.4 1.6 %copy.5 = bf16[256,256]{1,0:T(8,128)(2,1)} copy(bf16[256,256]{1,0:T(8,128)(2,1)} %purify.1) | data formatting | bytes 262144

commit v6 on v4

--- a/solution.py
+++ b/solution.py
@@ -20,6 +20,10 @@
     if stage == 4:
         return ((4, 0), (4, 1))
     return ((stage, 0), (8 - stage, 1), (stage, 1), (8 - stage, 0))
+
+
+def last(slot, half):
+    return slot == 4 or (slot, half) in ((3, 1), (5, 0))
 
 
 def kernel(
@@ -89,8 +93,8 @@
         downward = slot < 4 or (slot == 4 and half == 0)
         origin = slot - 1 if downward else (slot + 1) % 8
         z_ = below if downward else above
-        core_ = user(z_, 4) if slot == 4 else core
-        lane = jnp.where(core_ == core, 0, 1) if slot == 4 else 0
+        core_ = user(z_, slot) if last(slot, half) else core
+        lane = jnp.where(core_ == core, 0, 1) if last(slot, half) else 0
         src = left.at[step, 0, rows(half)] if origin == 0 else right.at[step, 0, origin, rows(half)]
         return remote(
             src, right.at[step, lane, slot, rows(half)],
@@ -190,6 +194,8 @@
         sib_left(step, 0).start()
         for stage in range(1, 4):
             for slot, half in order(stage):
+                if last(slot, half):
+                    continue
                 ring_copy(step, slot, half).wait_recv()
                 if stage < 3 or (slot == 3) == (half == 0):
                     ring_copy(step, slot + 1 if slot < 4 else slot - 1, half).start()
@@ -227,7 +233,11 @@
                     @pl.when(user(z, slot) == core)
                     def _():
                         for half in range(2):
-                            sib_copy(step, slot, half).wait_recv()
+                            if last(slot, half):
+                                for lane in range(2):
+                                    ring_arrival(step, lane, slot, half).wait_recv()
+                            else:
+                                sib_copy(step, slot, half).wait_recv()
                         multiply(step, slot)
 
         @pl.when(user(z, 4) == core)
@@ -269,7 +279,7 @@
         for slot in range(1, 8):
             for half in range(2):
                 ring_copy(step, slot, half).wait_send()
-                if slot != 4:
+                if not last(slot, half):
                     @pl.when(user(z, slot) != core)
                     def _():
                         sib_copy(step, slot, half).wait_send()

time: 61 us -> 60.6 us (level)
  no operation moved by 1% of the time
where the time goes in v6:
time: 60.6 us; the launch traced here: 60.5 us
  Pallas kernels  58.9 us (97%)
  local copies, waits for them, and re-layouts  1.57 us (3%)
    pallas_call x1, Pallas kernels, local(): pl.pallas_call(kernel, name='purify', out_shape=jax.ShapeDtypeStruct(bloc...  58.9 us
    unnamed x1, local copies, waits for them, and re-layouts  1.57 us

profile of v6, /device:TPU:1, one launch (start us, length us, event | category | flops | bytes accessed | tf_op | source)
XLA Modules:
  0.0 60.5 jit_solution(13283944442475149858)
XLA Ops:
  0.0 58.9 %purify.1 = bf16[256,256]{1,0:T(8,128)(2,1)} custom-call(s32[16,16]{1,0:T(8,128)} %start_hbm.1, s32[16,16]{1,0:T(8,128)} %square_hbm.1, bf16[256,256]{1,0:T(8,128)(2,1)} %density_hbm.1), custom_call_target="tpu_custom_call" | custom-call | tf_op jit(solution)/shard_map/purify/pallas_call | solution.py:309
  58.9 1.6 %copy.5 = bf16[256,256]{1,0:T(8,128)(2,1)} copy(bf16[256,256]{1,0:T(8,128)(2,1)} %purify.1) | data formatting | bytes 262144

commit v7 on v6

--- a/solution.py
+++ b/solution.py
@@ -74,8 +74,6 @@
         load.wait()
     left[0, 0, :BLOCK] = select_block(start_ref[row, col * 4 + x], density_ref[...])
     pl.semaphore_wait(barrier, len(partners))
-    for neighbour in beside:
-        pl.semaphore_signal(ready, inc=1, device_id=neighbour, device_id_type=MESH)
 
     def remote(src, dst, send, recv, target):
         return pltpu.make_async_remote_copy(
@@ -177,6 +175,8 @@
 
     for slot, half in order(1):
         ring_copy(0, slot, half).start()
+    for neighbour in beside:
+        pl.semaphore_signal(ready, inc=1, device_id=neighbour, device_id_type=MESH)
 
     @pl.when(yh != yl)
     def _():

time: 60.6 us -> 60.6 us (level)
  no operation moved by 1% of the time
where the time goes in v7:
time: 60.6 us; the launch traced here: 60.5 us
  Pallas kernels  58.9 us (97%)
  local copies, waits for them, and re-layouts  1.57 us (3%)
    pallas_call x1, Pallas kernels, local(): pl.pallas_call(kernel, name='purify', out_shape=jax.ShapeDtypeStruct(bloc...  58.9 us
    unnamed x1, local copies, waits for them, and re-layouts  1.57 us

profile of v7, /device:TPU:1, one launch (start us, length us, event | category | flops | bytes accessed | tf_op | source)
XLA Modules:
  0.0 60.5 jit_solution(3754036225649695204)
XLA Ops:
  0.0 58.9 %purify.1 = bf16[256,256]{1,0:T(8,128)(2,1)} custom-call(s32[16,16]{1,0:T(8,128)} %start_hbm.1, s32[16,16]{1,0:T(8,128)} %square_hbm.1, bf16[256,256]{1,0:T(8,128)(2,1)} %density_hbm.1), custom_call_target="tpu_custom_call" | custom-call | tf_op jit(solution)/shard_map/purify/pallas_call | solution.py:309
  58.9 1.6 %copy.5 = bf16[256,256]{1,0:T(8,128)(2,1)} copy(bf16[256,256]{1,0:T(8,128)(2,1)} %purify.1) | data formatting | bytes 262144
